TPU v7x, 256 devices: a whole 4x4x8 slice. The times are simulated.
256 devices in a mesh: gx: 16 (over y, x), gy: 16 (over z, core).
Axes of the slice: x: 4, y: 4, z: 8, core: 2. Of those that a mesh axis runs over, the one named last changes fastest.
Arguments:
- pressure: float32 [2, 2048, 2048], P(None, 'gx', 'gy'), may hold values from 0.5 to 1.5
- saturations: float32 [2, 2, 2048, 2048], P(None, None, 'gx', 'gy'), may hold values from 0.05 to 0.4
- old_mass: float32 [3, 2, 2048, 2048], P(None, None, 'gx', 'gy'), may hold values from 0 to 0.4
- pore_volume: float32 [2, 2048, 2048], P(None, 'gx', 'gy'), may hold values from 0.3 to 3
- transmissibility: float32 [3, 2, 2048, 2048], P(None, None, 'gx', 'gy'), may hold values from 0.3 to 3
- direction: float32 [3, 2, 2048, 2048], P(None, None, 'gx', 'gy'), may hold values from -6 to 6
- seg_pressure: float32 [512, 128], P('gx'), may hold values from 0.4 to 1.2
- seg_direction: float32 [512, 128], P('gx'), may hold values from -6 to 6
- perf_cell: int32 [512, 128], P('gx'), may hold values from 0 to 524287, as said below
- well_index: float32 [512, 128], P('gx'), may hold values from 0.2 to 2
- parent: int32 [512, 128], P('gx'), may hold values from 0 to 126, as said below
- seg_head: float32 [512, 128], P('gx'), may hold values from 0 to 0.3
- well_mode: int32 [512], P('gx'), may hold values from 0 to 1
- bhp_limit: float32 [512], P('gx'), may hold values from 0.3 to 0.8
- guide_rate: float32 [512], P('gx'), may hold values from 0.5 to 5
- group_of: int32 [512, 1], P('gx'), may hold values from 0 to 127
- group_target: float32 [128], replicated, may hold values from 200 to 800
Outputs:
- cell_residual: float32 [3, 2, 2048, 2048], P(None, None, 'gx', 'gy')
- cell_jvp: float32 [3, 2, 2048, 2048], P(None, None, 'gx', 'gy')
- seg_residual: float32 [512, 128], P(('gx', 'gy'))
- seg_jvp: float32 [512, 128], P(('gx', 'gy'))
- group_rates: float32 [3, 128], replicated
Inputs may be any that keep to these rules, and one draw needn't show every extreme that they name: perf_cell codes (layer * 128 + xl) * 2048 + row, with xl the column within the strip of 128 columns of the well's block of 32 wells. `parent`: segment 0 of every well names itself; every other segment names a segment of lower number. `group_of`: every group has at least one well.
All inputs are finite; a program needn't handle non-finite values.
Results may differ from a plain program's by a relative error of at most 0.0003.
Values sent between devices are 32-bit elements; how exact they have to be, the bound alone decides.
A program may use at most 128 MiB of HBM per device.

v0:
```python
import jax
import jax.numpy as jnp
from jax import lax
from jax.sharding import PartitionSpec as P

COMPRESS = (0.05, 0.2, 1.0)
VISCOSITY = (0.5, 1.0, 0.2)
DENSITY = (1.0, 0.8, 0.2)
ROCK_COMP = 0.01
GRAVITY = 0.05
UPWIND_WIDTH = 0.02
FRICTION = 0.002
RATE_SCALE = 0.1


def padded_2(x, sides, width):
    for axis, dim in sides:
        devices, length = (lax.axis_size(axis), x.shape[dim])
        up = [(i, (i + 1) % devices) for i in range(devices - 1)]
        down = [(j, i) for i, j in up]
        last = lax.slice_in_dim(x, length - width, length, axis=dim)
        first = lax.slice_in_dim(x, 0, width, axis=dim)
        before = lax.ppermute(last, axis, up)
        after = lax.ppermute(first, axis, down)
        x = jnp.concatenate([before, x, after], axis=dim)
    return x


def phase_props(press, water, gas):
    oil = 1.0 - water - gas
    satur = (water, oil, gas)
    rock = 1.0 + ROCK_COMP * (press - 1.0)
    mobility = []
    masses = []
    for phase in range(3):
        volume = jnp.exp(COMPRESS[phase] * (press - 1.0))
        mobility.append(satur[phase] * satur[phase] * volume / VISCOSITY[phase])
        masses.append(rock * satur[phase] * volume)
    return (jnp.stack(mobility), jnp.stack(masses))


def face_flux(press_in, press_out, mobil_in, mobil_out, trans, lift):
    fluxes = []
    for phase in range(3):
        potential = press_in - press_out + DENSITY[phase] * lift
        upwind = jax.nn.sigmoid(potential / UPWIND_WIDTH)
        fluxes.append(
            trans * (upwind * mobil_in[phase] + (1.0 - upwind) * mobil_out[phase]) * potential
        )
    return jnp.stack(fluxes)


def ancestry(parent):
    count = parent.shape[1]
    segment_ids = jnp.arange(count, dtype=jnp.int32)
    reach = (segment_ids[None, :, None] == segment_ids[None, None, :]) | (
        parent[:, None, :] == segment_ids[None, :, None]
    )
    reach = reach.astype(jnp.bfloat16)
    for level in range((count - 1).bit_length()):
        product = jnp.einsum("wsu,wut->wst", reach, reach, preferred_element_type=jnp.float32)
        reach = jnp.minimum(product, 1.0).astype(jnp.bfloat16)
    return reach.astype(jnp.float32)


def segment_terms(parent, seg_head, well_mode, bhp_limit, target):
    reach = ancestry(parent)

    def equations(total_vals, seg_vals):
        flow = jnp.einsum("wst,wt->ws", reach, total_vals, precision=lax.Precision.HIGHEST)
        above = jnp.take_along_axis(seg_vals, parent, axis=1)
        inner = seg_vals - above - seg_head - FRICTION * flow
        root = jnp.where(
            well_mode == 1, RATE_SCALE * (flow[:, 0] - target), seg_vals[:, 0] - bhp_limit
        )
        return inner.at[:, 0].set(root)

    return equations


def per_device(
    pressure,
    saturations,
    old_mass,
    pore_volume,
    transmissibility,
    direction,
    seg_pressure,
    seg_direction,
    perf_cell,
    well_index,
    parent,
    seg_head,
    well_mode,
    bhp_limit,
    guide_rate,
    group_of,
    group_target,
):
    layers, cols, rows = pressure.shape
    col_count = lax.axis_size("gx")
    row_count = lax.axis_size("gy")
    col_index = lax.axis_index("gx")
    row_index = lax.axis_index("gy")
    col_glob = col_index * cols + jnp.arange(cols, dtype=jnp.int32)
    row_glob = row_index * rows + jnp.arange(rows, dtype=jnp.int32)
    trans_cols = jnp.where(
        (col_glob == cols * col_count - 1)[None, :, None], 0.0, transmissibility[0]
    )
    trans_rows = jnp.where(
        (row_glob == rows * row_count - 1)[None, None, :], 0.0, transmissibility[1]
    )
    stacked = jnp.concatenate(
        [pressure[None], saturations, direction, trans_cols[None], trans_rows[None]], axis=0
    )
    padded = padded_2(stacked, (("gx", 2), ("gy", 3)), 1)
    state_pad = padded[0:3]
    direc_pad = padded[3:6]
    tcol_pad = padded[6]
    trow_pad = padded[7]
    all_rows = rows * row_count
    layer_span = cols * all_rows
    layer = perf_cell // layer_span
    remain = perf_cell % layer_span
    local_row = remain % all_rows - row_index * rows
    owned = (local_row >= 0) & (local_row < rows)
    flat_cell = (layer * cols + remain // all_rows) * rows + jnp.clip(local_row, 0, rows - 1)
    weight = jnp.where(owned, well_index, 0.0)

    def local_terms(state, seg_vals):
        press = state[0]
        mobility, masses = phase_props(press, state[1], state[2])
        mobil_in = mobility[:, :, 1:-1, 1:-1]
        press_in = press[:, 1:-1, 1:-1]
        residual = masses[:, :, 1:-1, 1:-1] * pore_volume - old_mass
        flux_cols = face_flux(
            press[:, :-1, 1:-1],
            press[:, 1:, 1:-1],
            mobility[:, :, :-1, 1:-1],
            mobility[:, :, 1:, 1:-1],
            tcol_pad[:, :-1, 1:-1],
            0.0,
        )
        residual = residual + flux_cols[:, :, 1:] - flux_cols[:, :, :-1]
        flux_rows = face_flux(
            press[:, 1:-1, :-1],
            press[:, 1:-1, 1:],
            mobility[:, :, 1:-1, :-1],
            mobility[:, :, 1:-1, 1:],
            trow_pad[:, 1:-1, :-1],
            0.0,
        )
        residual = residual + flux_rows[:, :, :, 1:] - flux_rows[:, :, :, :-1]
        flux_layers = face_flux(
            press_in[:-1],
            press_in[1:],
            mobil_in[:, :-1],
            mobil_in[:, 1:],
            transmissibility[2][:-1],
            GRAVITY,
        )
        residual = (
            residual
            + jnp.pad(flux_layers, ((0, 0), (0, 1), (0, 0), (0, 0)))
            - jnp.pad(flux_layers, ((0, 0), (1, 0), (0, 0), (0, 0)))
        )
        mobil_flat = mobil_in.reshape(3, -1)
        rates = weight * mobil_flat[:, flat_cell] * (press_in.reshape(-1)[flat_cell] - seg_vals)
        residual = (
            residual.reshape(3, -1)
            .at[:, flat_cell.reshape(-1)]
            .add(rates.reshape(3, -1))
            .reshape(residual.shape)
        )
        return (residual, rates)

    primal, tangent = jax.jvp(local_terms, (state_pad, seg_pressure), (direc_pad, seg_direction))
    cell_residual, rates = primal
    cell_jvp, rate_tangent = tangent
    rate_total = jnp.sum(rates, axis=0)
    total_tangent = jnp.sum(rate_tangent, axis=0)
    member = (
        group_of[:, 0][:, None] == jnp.arange(group_target.shape[0], dtype=jnp.int32)[None, :]
    ).astype(jnp.float32)
    rates_part = jnp.dot(jnp.sum(rates, axis=2), member, precision=lax.Precision.HIGHEST)
    guide_part = jnp.dot(guide_rate, member, precision=lax.Precision.HIGHEST)
    guide_total = lax.psum(guide_part, "gx")
    group_rates = lax.psum(rates_part, ("gx", "gy"))
    target = (
        jnp.dot(member, group_target, precision=lax.Precision.HIGHEST)
        * guide_rate
        / jnp.dot(member, guide_total, precision=lax.Precision.HIGHEST)
    )
    well_count = seg_pressure.shape[0]
    share = well_count // row_count
    start = row_index * share

    def pick(values):
        return lax.dynamic_slice_in_dim(values, start, share, 0)

    total_sum, tangent_sum = lax.psum((rate_total, total_tangent), "gy")
    equations = segment_terms(parent, seg_head, well_mode, bhp_limit, target)
    seg_full, seg_tan = jax.jvp(equations, (total_sum, seg_pressure), (tangent_sum, seg_direction))
    seg_residual = pick(seg_full)
    seg_jvp = pick(seg_tan)
    return (cell_residual, cell_jvp, seg_residual, seg_jvp, group_rates)


def solution(mesh):
    placed = (
        P(None, "gx", "gy"),
        P(None, None, "gx", "gy"),
        P(None, None, "gx", "gy"),
        P(None, "gx", "gy"),
        P(None, None, "gx", "gy"),
        P(None, None, "gx", "gy"),
        P("gx", None),
        P("gx", None),
        P("gx", None),
        P("gx", None),
        P("gx", None),
        P("gx", None),
        P("gx"),
        P("gx"),
        P("gx"),
        P("gx", None),
        P(),
    )
    return jax.shard_map(
        per_device,
        mesh=mesh,
        in_specs=placed,
        out_specs=(
            P(None, None, "gx", "gy"),
            P(None, None, "gx", "gy"),
            P(("gx", "gy"), None),
            P(("gx", "gy"), None),
            P(),
        ),
        check_vma=False,
    )
```

profile of v0, /device:TPU:1, one launch (start us, length us, event | category | flops | bytes accessed | tf_op | source)
XLA Modules:
  0.0 510.7 jit_solution(14686973665699037031)
XLA Ops:
  0.7 0.9 bitcast_dynamic-update-slice_fusion
  1.7 1.0 constant_dynamic-update-slice_fusion.1
  2.6 1.0 constant_dynamic-update-slice_fusion
  3.7 1.0 select_dynamic-update-slice_fusion.1
  4.7 0.9 select_dynamic-update-slice_fusion
  5.6 1.3 collective-permute-start.1
  6.9 4.6 collective-permute-start
  11.6 0.6 compare_select_fusion
  12.2 0.8 minimum_convert_fusion.6
  13.0 1.0 minimum_convert_fusion.4
  14.0 1.0 minimum_convert_fusion.2
  15.0 2.0 minimum_convert_fusion
  17.2 32.3 %psum.29 = f32[128]{0:T(128)S(1)} all-reduce(f32[128]{0:T(128)S(1)} %convolution_bitcast_fusion.1), channel_id=1, replica_groups=mesh['gx'=16,'gy'=16] {'gx'}, use_global_device_ids=true, to_apply=%region_5.6 | all-reduce | flops 128 | bytes 1024 | tf_op jit(solution)/shard_map/psum | solution.py:187
  49.5 0.7 convolution_bitcast_fusion
  50.2 0.6 slice_reduce_fusion.2
  50.9 0.4 fusion.172
  51.3 0.6 copy.106
  51.9 9.9 %collective-permute-start.3 = (f32[8,2,130,1]{2,0,3,1:T(8,128)S(1)}, f32[8,2,130,1]{2,0,3,1:T(8,128)S(1)}, u32[]{:S(2)}, u32[]{:S(2)}) collective-permute-start(f32[8,2,130,1]{2,0,3,1:T(8,128)S(1)} %copy.106), channel_id=1, source_target_pairs={{1,0},{2,1},{3,2},{4,3},{5,4},{6,5},{7,6},{8,7},{9,8},{10,9},{11,1... | collective-permute-start | bytes 24968 | tf_op jit(solution)/shard_map/ppermute | solution.py:24
  61.8 0.6 copy.105
  62.4 3.6 collective-permute-start.2
  66.2 43.2 %gather_fusion.5 = f32[4096]{0:T(1024)} fusion(f32[32,128]{1,0:T(8,128)S(1)} %copy-done.1, s32[4096]{0:T(1024)S(1)} %fusion.156), kind=kCustom, calls=%fused_computation.5 | custom fusion | bytes 65536 | tf_op jit(solution)/shard_map/jvp(jit(take_along_axis))/gather | solution.py:71
  109.4 25.6 %gather_fusion.4 = f32[4096]{0:T(1024)S(1)} fusion(f32[32,128]{1,0:T(8,128)S(1)} %copy-done.2, s32[4096]{0:T(1024)S(1)} %fusion.156), kind=kCustom, calls=%fused_computation.4 | custom fusion | bytes 65536 | tf_op jit(solution)/shard_map/jvp(jit(take_along_axis))/gather | solution.py:71
  135.0 0.6 compare_reduce_fusion
  135.7 0.4 copy.108
  136.1 0.4 copy.107
  136.5 1.0 pad_maximum_fusion
  137.6 0.3 fusion.38
  138.1 1.2 fusion.39
  139.3 0.5 fusion.54
  139.8 0.4 fusion.89
  140.2 0.3 multiply_bitcast_fusion.2
  140.5 0.2 multiply_bitcast_fusion.5
  140.7 0.7 fusion.60
  141.4 0.5 fusion.95
  141.9 0.2 fusion.118
  142.1 0.3 fusion.127
  142.5 0.3 pad_maximum_fusion.6
  143.0 1.0 pad_maximum_fusion.2
  144.1 0.7 pad_maximum_fusion.14
  144.8 0.3 fusion.34
  145.2 8.6 %copy.109 = f32[3,2,128,128]{0,3,2,1:T(8,128)} copy(f32[3,2,128,128]{3,2,1,0:T(8,128)S(1)} %fusion.34) | data formatting | bytes 786432 | tf_op jit(solution)/shard_map/jvp()/sub | solution.py:163
  153.7 8.5 %copy.110 = f32[3,2,128,128]{0,3,2,1:T(8,128)} copy(f32[3,2,128,128]{3,2,1,0:T(8,128)S(1)} %get-tuple-element.106) | data formatting | bytes 786432 | tf_op jit(solution)/shard_map/jvp()/slice | solution.py:133
  162.2 16.5 %gather_fusion = f32[4096,3]{1,0:T(8,128)S(1)} fusion(f32[3,32768]{0,1:T(8,128)} %bitcast.414, s32[4096]{0:T(1024)S(1)} %get-tuple-element.69), kind=kCustom, calls=%fused_computation | custom fusion | bytes 114688 | tf_op jit(solution)/shard_map/jvp()/gather | solution.py:168
  178.8 40.6 %gather_fusion.3 = f32[4096]{0:T(1024)} fusion(f32[32768]{0:T(1024)S(1)} %bitcast.407, s32[4096]{0:T(1024)S(1)} %get-tuple-element.69), kind=kCustom, calls=%fused_computation.3 | custom fusion | bytes 49152 | tf_op jit(solution)/shard_map/jvp()/gather | solution.py:168
  219.4 23.0 %gather_fusion.1 = f32[4096]{0:T(1024)S(1)} fusion(f32[32768]{0:T(1024)S(1)} %bitcast.408, s32[4096]{0:T(1024)S(1)} %get-tuple-element.69), kind=kCustom, calls=%fused_computation.1 | custom fusion | bytes 49152 | tf_op jit(solution)/shard_map/jvp()/gather | solution.py:168
  242.4 36.5 %scatter_custom_fusion = f32[3,32768]{0,1:T(8,128)} fusion(f32[3,32768]{0,1:T(8,128)} %bitcast.409, s32[4096]{0:T(1024)} %bitcast.429, f32[4096,3]{1,0:T(8,128)S(1)} %gather_fusion, f32[4096]{0:T(1024)S(1)} %bitcast.419, f32[4096]{0:T(1024)S(1)} %bitcast.417), kind=kCustom, calls=%fused_computation.15 | custom fusion | flops 36864 | bytes 475136 | tf_op jit(solution)/shard_map/jvp()/scatter-add | solution.py:172
  278.9 10.7 %copy.115 = f32[3,2,128,128]{3,2,1,0:T(8,128)} copy(f32[3,2,128,128]{0,3,2,1:T(8,128)} %bitcast.410) | data formatting | bytes 786432
  289.6 2.5 fusion.31
  292.1 9.5 %copy.111 = f32[3,2,128,128]{0,3,2,1:T(8,128)} copy(f32[3,2,128,128]{3,2,1,0:T(8,128)} %fusion.31) | data formatting | bytes 786432 | tf_op jit(solution)/shard_map/jvp()/sub | solution.py:163
  301.6 8.5 %copy.112 = f32[3,2,128,128]{0,3,2,1:T(8,128)} copy(f32[3,2,128,128]{3,2,1,0:T(8,128)S(1)} %get-tuple-element.105) | data formatting | bytes 786432 | tf_op jit(solution)/shard_map/jvp()/slice | solution.py:133
  310.1 19.9 %gather_fusion.2 = f32[4096,3]{1,0:T(8,128)} fusion(f32[3,32768]{0,1:T(8,128)} %bitcast.415, s32[4096]{0:T(1024)S(1)} %get-tuple-element.69), kind=kCustom, calls=%fused_computation.2 | custom fusion | bytes 114688 | tf_op jit(solution)/shard_map/jvp()/gather | solution.py:168
  330.1 37.0 %scatter_custom_fusion.1 = f32[3,32768]{0,1:T(8,128)} fusion(f32[3,32768]{0,1:T(8,128)} %bitcast.411, s32[4096]{0:T(1024)} %bitcast.430, f32[4096,3]{1,0:T(8,128)} %gather_fusion.2, f32[4096,3]{1,0:T(8,128)S(1)} %gather_fusion, f32[4096]{0:T(1024)S(1)} %bitcast.425, f32[4096]{0:T(1024)S(1)} %bitcast.420, f32[4096]{0:T(1024)S(1)} %bitcast.418), kind=kCustom, calls=%fused_computation.13 | custom fusion | flops 73728 | bytes 2588672 | tf_op jit(solution)/shard_map/jvp()/scatter-add | solution.py:172
  367.0 10.6 %copy.116 = f32[3,2,128,128]{3,2,1,0:T(8,128)} copy(f32[3,2,128,128]{0,3,2,1:T(8,128)} %bitcast.412) | data formatting | bytes 786432
  377.7 4.6 add_reduce_fusion
  382.4 46.0 %all-reduce.4 = (f32[32,128]{1,0:T(8,128)S(1)}, f32[32,128]{1,0:T(8,128)S(1)}) all-reduce(f32[32,128]{1,0:T(8,128)S(1)} %get-tuple-element.55, f32[32,128]{1,0:T(8,128)S(1)} %get-tuple-element.54), channel_id=1, replica_groups=mesh['gx'=16,'gy'=16] {'gy'}, use_global_device_ids=true, to_apply=%region_3.4 | all-reduce | flops 8192 | bytes 65536 | tf_op jit(solution)/shard_map/psum | solution.py:201
  428.4 1.7 fusion.175
  430.2 1.7 fusion.174
  432.2 0.2 fusion.19
  432.5 0.7 slice_select_fusion.1
  433.4 0.6 slice_select_fusion
  434.1 0.6 constant_dynamic-slice_fusion.1
  434.7 0.6 constant_dynamic-slice_fusion
  435.3 0.2 fusion.157
  435.5 75.3 %psum.31 = f32[3,128]{1,0:T(4,128)} all-reduce(f32[3,128]{1,0:T(4,128)S(1)} %fusion.157), channel_id=1, replica_groups=mesh['gx'=16,'gy'=16] {'gx','gy'}, use_global_device_ids=true, to_apply=%region_9.10 | all-reduce | flops 384 | bytes 3072 | tf_op jit(solution)/shard_map/psum | solution.py:188
  (73 shorter events, 1.9 us)
Async XLA Ops:
  0.6 431.5 %copy-start = (f32[128]{0:T(128)S(1)}, f32[128]{0:T(128)}, u32[]{:S(2)}) copy-start(f32[128]{0:T(128)} %param.37) | copy-start | bytes 1540
  0.6 10.9 %copy-start.8 = (s32[32,128]{1,0:T(8,128)S(1)}, s32[32,128]{1,0:T(8,128)}, u32[]{:S(2)}) copy-start(s32[32,128]{1,0:T(8,128)} %param.29) | copy-start | bytes 49156
  0.7 11.5 %copy-start.12 = (f32[32,128]{1,0:T(8,128)S(1)}, f32[32,128]{1,0:T(8,128)}, u32[]{:S(2)}) copy-start(f32[32,128]{1,0:T(8,128)} %param.30) | copy-start | bytes 49156
  0.7 11.5 %copy-start.9 = (s32[32,128]{1,0:T(8,128)S(1)}, s32[32,128]{1,0:T(8,128)}, u32[]{:S(2)}) copy-start(s32[32,128]{1,0:T(8,128)} %param.31) | copy-start | bytes 49156
  5.6 45.2 %collective-permute-start.1 = (f32[8,2,1,128]{3,2,1,0:T(1,128)S(1)}, f32[8,2,1,128]{3,2,1,0:T(1,128)S(1)}, u32[]{:S(2)}, u32[]{:S(2)}) collective-permute-start(f32[8,2,1,128]{3,2,1,0:T(1,128)S(1)} %get-tuple-element.89), channel_id=1, source_target_pairs={{16,0},{32,16},{48,32},{64,48},{80,64},{96,80},{112,96},{128,112},... | collective-permute-start | bytes 24584 | tf_op jit(solution)/shard_map/ppermute | solution.py:24
  6.9 43.9 %collective-permute-start = (f32[8,2,1,128]{3,2,1,0:T(1,128)S(1)}, f32[8,2,1,128]{3,2,1,0:T(1,128)S(1)}, u32[]{:S(2)}, u32[]{:S(2)}) collective-permute-start(f32[8,2,1,128]{3,2,1,0:T(1,128)S(1)} %get-tuple-element.88), channel_id=1, source_target_pairs={{0,16},{16,32},{32,48},{48,64},{64,80},{80,96},{96,112},{112,128},... | collective-permute-start | bytes 24584 | tf_op jit(solution)/shard_map/ppermute | solution.py:23
  15.0 2.0 copy-start.16
  15.0 2.0 copy-start.19
  15.0 35.2 %copy-start.2 = (f32[32,128]{1,0:T(8,128)S(1)}, f32[32,128]{1,0:T(8,128)}, u32[]{:S(2)}) copy-start(f32[32,128]{1,0:T(8,128)} %param.27) | copy-start | bytes 49156
  51.3 14.8 %copy-start.1 = (f32[32,128]{1,0:T(8,128)S(1)}, f32[32,128]{1,0:T(8,128)}, u32[]{:S(2)}) copy-start(f32[32,128]{1,0:T(8,128)} %param.28) | copy-start | bytes 49156
  51.9 83.8 %collective-permute-start.3 = (f32[8,2,130,1]{2,0,3,1:T(8,128)S(1)}, f32[8,2,130,1]{2,0,3,1:T(8,128)S(1)}, u32[]{:S(2)}, u32[]{:S(2)}) collective-permute-start(f32[8,2,130,1]{2,0,3,1:T(8,128)S(1)} %copy.106), channel_id=1, source_target_pairs={{1,0},{2,1},{3,2},{4,3},{5,4},{6,5},{7,6},{8,7},{9,8},{10,9},{11,1... | collective-permute-start | bytes 24968 | tf_op jit(solution)/shard_map/ppermute | solution.py:24
  62.4 73.7 %collective-permute-start.2 = (f32[8,2,130,1]{2,0,3,1:T(8,128)S(1)}, f32[8,2,130,1]{2,0,3,1:T(8,128)S(1)}, u32[]{:S(2)}, u32[]{:S(2)}) collective-permute-start(f32[8,2,130,1]{2,0,3,1:T(8,128)S(1)} %copy.105), channel_id=1, source_target_pairs={{0,1},{1,2},{2,3},{3,4},{4,5},{5,6},{6,7},{7,8},{8,9},{9,10},{10,1... | collective-permute-start | bytes 24968 | tf_op jit(solution)/shard_map/ppermute | solution.py:23
  140.7 1.2 copy-start.5
  143.0 1.8 copy-start.6
  143.0 1.8 copy-start.7
  219.4 23.0 %copy-start.11 = (f32[4096]{0:T(1024)S(1)}, f32[4096]{0:T(1024)}, u32[]{:S(2)}) copy-start(f32[4096]{0:T(1024)} %gather_fusion.3) | copy-start | bytes 49156
  278.9 10.7 %copy-start.4 = (f32[3,1,128,128]{3,2,1,0:T(8,128)S(1)}, f32[3,1,128,128]{3,2,1,0:T(8,128)}, u32[]{:S(2)}) copy-start(f32[3,1,128,128]{3,2,1,0:T(8,128)} %get-tuple-element.112) | copy-start | bytes 589828
  377.7 50.7 %copy-start.3 = (bf16[32,128,128]{2,1,0:T(8,128)(2,1)S(1)}, bf16[32,128,128]{2,1,0:T(8,128)(2,1)}, u32[]{:S(2)}) copy-start(bf16[32,128,128]{2,1,0:T(8,128)(2,1)} %minimum_convert_fusion) | copy-start | bytes 3145732
  377.7 52.5 %copy-start.10 = (f32[4096]{0:T(1024)S(1)}, f32[4096]{0:T(1024)}, u32[]{:S(2)}) copy-start(f32[4096]{0:T(1024)} %gather_fusion.5) | copy-start | bytes 49156
  382.3 49.8 %copy-start.14 = (f32[32]{0:T(128)S(1)}, f32[32]{0:T(128)}, u32[]{:S(2)}) copy-start(f32[32]{0:T(128)} %slice_reduce_fusion.2) | copy-start | bytes 388
  382.3 49.8 %copy-start.15 = (s32[32]{0:T(128)S(1)}, s32[32]{0:T(128)}, u32[]{:S(2)}) copy-start(s32[32]{0:T(128)} %param.33) | copy-start | bytes 388
  382.3 49.8 %copy-start.17 = (f32[32]{0:T(128)S(1)}, f32[32]{0:T(128)}, u32[]{:S(2)}) copy-start(f32[32]{0:T(128)} %param.35) | copy-start | bytes 388
  382.3 49.8 %copy-start.18 = (f32[32]{0:T(128)S(1)}, f32[32]{0:T(128)}, u32[]{:S(2)}) copy-start(f32[32]{0:T(128)} %param.34) | copy-start | bytes 388
  382.4 49.8 %copy-start.20 = (s32[32,1]{0,1:T(1,128)S(1)}, s32[32,1]{0,1:T(1,128)}, u32[]{:S(2)}) copy-start(s32[32,1]{0,1:T(1,128)} %param.36) | copy-start | bytes 388
  382.4 49.8 %copy-start.21 = (f32[32]{0:T(128)S(1)}, f32[32]{0:T(128)}, u32[]{:S(2)}) copy-start(f32[32]{0:T(128)} %convolution_bitcast_fusion) | copy-start | bytes 388
  382.4 50.1 %copy-start.13 = (f32[32,128]{1,0:T(8,128)S(1)}, f32[32,128]{1,0:T(8,128)}, u32[]{:S(2)}) copy-start(f32[32,128]{1,0:T(8,128)} %param.32) | copy-start | bytes 49156
where the time goes:
time: 512 us; the launch traced here: 511 us
  local copies, waits for them, and re-layouts  233 us (46%)
  blocking collectives  154 us (30%)
  other arithmetic  93.7 us (18%)
  starting transfers between devices  19.4 us (4%)
  matrix products  9.4 us (2%)
    psum x1, blocking collectives, per_device(): group_rates = lax.psum(rates_part, ('gx', 'gy'))  75.3 us
    scatter-add x2, other arithmetic, local_terms(): residual = residual.reshape(3, -1).at[:, flat_cell.reshape(-1)].add(rates...  73.5 us
    gather x2, local copies, waits for them, and re-layouts, equations(): above = jnp.take_along_axis(seg_vals, parent, axis=1)  68.8 us
    gather x2, local copies, waits for them, and re-layouts, local_terms(): press_in.reshape(-1)[flat_cell] - seg_vals  63.6 us
    psum x1, blocking collectives, per_device(): total_sum, tangent_sum = lax.psum((rate_total, total_tangent), 'gy')  46 us
    gather x2, local copies, waits for them, and re-layouts, local_terms(): mobil_flat[:, flat_cell]  36.5 us
    psum x1, blocking collectives, per_device(): guide_total = lax.psum(guide_part, 'gx')  32.3 us
    unnamed x49, local copies, waits for them, and re-layouts  24.4 us
  transfers between devices with their start and end apart: 4, of which 0 were waited for; matrix products, arithmetic and copies ran while one was open for 15% of the time, Pallas kernels for 0%

commit v1 on v0

--- a/solution.py
+++ b/solution.py
@@ -185,7 +185,9 @@
     rates_part = jnp.dot(jnp.sum(rates, axis=2), member, precision=lax.Precision.HIGHEST)
     guide_part = jnp.dot(guide_rate, member, precision=lax.Precision.HIGHEST)
     guide_total = lax.psum(guide_part, "gx")
-    group_rates = lax.psum(rates_part, ("gx", "gy"))
+    group_rates = rates_part
+    for over in ("gy", "gx"):
+        group_rates = lax.psum(group_rates, over)
     target = (
         jnp.dot(member, group_target, precision=lax.Precision.HIGHEST)
         * guide_rate

time: 512 us -> 437 us (0.85); the launches traced: 511 us -> 429 us
  blocking collectives: 154 us -> 78 us
  starting transfers between devices: 19.4 us -> 13.1 us
    psum x1 -> x0, blocking collectives: 75.3 us -> none  [per_device(): group_rates = lax.psum(rates_part, ('gx', 'gy'))]
  transfers between devices with their start and end apart: 4 -> 4, of which waited for: 0 -> 0; matrix products, arithmetic and copies ran while one was open for 15% -> 18% of each run, Pallas kernels for 0% -> 0%
where the time goes in v1:
time: 437 us; the launch traced here: 429 us
  local copies, waits for them, and re-layouts  234 us (54%)
  other arithmetic  93.7 us (21%)
  blocking collectives  78 us (18%)
  starting transfers between devices  13.1 us (3%)
  matrix products  9.38 us (2%)
    scatter-add x2, other arithmetic, local_terms(): residual = residual.reshape(3, -1).at[:, flat_cell.reshape(-1)].add(rates...  73.5 us
    gather x2, local copies, waits for them, and re-layouts, equations(): above = jnp.take_along_axis(seg_vals, parent, axis=1)  68.8 us
    gather x2, local copies, waits for them, and re-layouts, local_terms(): press_in.reshape(-1)[flat_cell] - seg_vals  63.6 us
    psum x1, blocking collectives, per_device(): total_sum, tangent_sum = lax.psum((rate_total, total_tangent), 'gy')  45.6 us
    gather x2, local copies, waits for them, and re-layouts, local_terms(): mobil_flat[:, flat_cell]  36.5 us
    psum x1, blocking collectives, per_device(): guide_total = lax.psum(guide_part, 'gx')  32.3 us
    unnamed x49, local copies, waits for them, and re-layouts  24.4 us
    sub x2, local copies, waits for them, and re-layouts, local_terms(): residual + jnp.pad(flux_layers, ((0, 0), (0, 1), (0, 0), (0, 0)))  18.1 us
  transfers between devices with their start and end apart: 4, of which 0 were waited for; matrix products, arithmetic and copies ran while one was open for 18% of the time, Pallas kernels for 0%

profile of v1, /device:TPU:1, one launch (start us, length us, event | category | flops | bytes accessed | tf_op | source)
XLA Modules:
  0.0 428.9 jit_solution(16992147838126183002)
XLA Ops:
  0.7 0.9 bitcast_dynamic-update-slice_fusion
  1.7 1.0 constant_dynamic-update-slice_fusion.1
  2.6 1.0 constant_dynamic-update-slice_fusion
  3.7 1.0 select_dynamic-update-slice_fusion.1
  4.7 0.9 select_dynamic-update-slice_fusion
  5.6 1.3 collective-permute-start.1
  6.9 4.6 %collective-permute-start = (f32[8,2,1,128]{3,2,1,0:T(1,128)S(1)}, f32[8,2,1,128]{3,2,1,0:T(1,128)S(1)}, u32[]{:S(2)}, u32[]{:S(2)}) collective-permute-start(f32[8,2,1,128]{3,2,1,0:T(1,128)S(1)} %get-tuple-element.91), channel_id=1, source_target_pairs={{0,16},{16,32},{32,48},{48,64},{64,80},{80,96},{96,112},{112,128},... | collective-permute-start | bytes 24584 | tf_op jit(solution)/shard_map/ppermute | solution.py:23
  11.6 0.6 compare_select_fusion
  12.2 0.8 minimum_convert_fusion.6
  13.0 1.0 minimum_convert_fusion.4
  14.0 1.0 minimum_convert_fusion.2
  15.0 2.0 minimum_convert_fusion
  17.0 0.7 convolution_bitcast_fusion.1
  17.7 0.6 slice_reduce_fusion.2
  18.4 0.4 fusion.172
  18.8 0.6 copy.106
  19.4 5.1 %collective-permute-start.3 = (f32[8,2,130,1]{2,0,3,1:T(8,128)S(1)}, f32[8,2,130,1]{2,0,3,1:T(8,128)S(1)}, u32[]{:S(2)}, u32[]{:S(2)}) collective-permute-start(f32[8,2,130,1]{2,0,3,1:T(8,128)S(1)} %copy.106), channel_id=1, source_target_pairs={{1,0},{2,1},{3,2},{4,3},{5,4},{6,5},{7,6},{8,7},{9,8},{10,9},{11,1... | collective-permute-start | bytes 24968 | tf_op jit(solution)/shard_map/ppermute | solution.py:24
  24.5 0.6 copy.105
  25.1 2.1 collective-permute-start.2
  27.4 43.2 %gather_fusion.5 = f32[4096]{0:T(1024)} fusion(f32[32,128]{1,0:T(8,128)S(1)} %copy-done.1, s32[4096]{0:T(1024)S(1)} %fusion.156), kind=kCustom, calls=%fused_computation.5 | custom fusion | bytes 65536 | tf_op jit(solution)/shard_map/jvp(jit(take_along_axis))/gather | solution.py:71
  70.5 25.6 %gather_fusion.4 = f32[4096]{0:T(1024)S(1)} fusion(f32[32,128]{1,0:T(8,128)S(1)} %copy-done.2, s32[4096]{0:T(1024)S(1)} %fusion.156), kind=kCustom, calls=%fused_computation.4 | custom fusion | bytes 65536 | tf_op jit(solution)/shard_map/jvp(jit(take_along_axis))/gather | solution.py:71
  96.2 0.7 compare_reduce_fusion
  96.9 0.4 copy.108
  97.3 0.4 copy.107
  97.7 1.0 pad_maximum_fusion
  98.8 0.3 fusion.38
  99.0 0.2 multiply_add_fusion.1
  99.2 1.2 fusion.39
  100.5 0.5 fusion.54
  101.0 0.4 fusion.89
  101.4 0.3 multiply_bitcast_fusion.2
  101.7 0.2 multiply_bitcast_fusion.5
  101.9 0.7 fusion.60
  102.6 0.5 fusion.95
  103.1 0.2 fusion.118
  103.3 0.3 fusion.127
  103.7 0.3 pad_maximum_fusion.6
  104.2 1.0 pad_maximum_fusion.2
  105.3 0.7 pad_maximum_fusion.14
  106.0 0.3 fusion.34
  106.4 8.6 %copy.109 = f32[3,2,128,128]{0,3,2,1:T(8,128)} copy(f32[3,2,128,128]{3,2,1,0:T(8,128)S(1)} %fusion.34) | data formatting | bytes 786432 | tf_op jit(solution)/shard_map/jvp()/sub | solution.py:163
  114.9 8.6 %copy.110 = f32[3,2,128,128]{0,3,2,1:T(8,128)} copy(f32[3,2,128,128]{3,2,1,0:T(8,128)S(1)} %get-tuple-element.109) | data formatting | bytes 786432 | tf_op jit(solution)/shard_map/jvp()/slice | solution.py:133
  123.5 16.5 %gather_fusion = f32[4096,3]{1,0:T(8,128)S(1)} fusion(f32[3,32768]{0,1:T(8,128)} %bitcast.414, s32[4096]{0:T(1024)S(1)} %get-tuple-element.72), kind=kCustom, calls=%fused_computation | custom fusion | bytes 114688 | tf_op jit(solution)/shard_map/jvp()/gather | solution.py:168
  140.0 40.6 %gather_fusion.3 = f32[4096]{0:T(1024)} fusion(f32[32768]{0:T(1024)S(1)} %bitcast.407, s32[4096]{0:T(1024)S(1)} %get-tuple-element.72), kind=kCustom, calls=%fused_computation.3 | custom fusion | bytes 49152 | tf_op jit(solution)/shard_map/jvp()/gather | solution.py:168
  180.6 23.0 %gather_fusion.1 = f32[4096]{0:T(1024)S(1)} fusion(f32[32768]{0:T(1024)S(1)} %bitcast.408, s32[4096]{0:T(1024)S(1)} %get-tuple-element.72), kind=kCustom, calls=%fused_computation.1 | custom fusion | bytes 49152 | tf_op jit(solution)/shard_map/jvp()/gather | solution.py:168
  203.7 36.5 %scatter_custom_fusion = f32[3,32768]{0,1:T(8,128)} fusion(f32[3,32768]{0,1:T(8,128)} %bitcast.409, s32[4096]{0:T(1024)} %bitcast.429, f32[4096,3]{1,0:T(8,128)S(1)} %gather_fusion, f32[4096]{0:T(1024)S(1)} %bitcast.419, f32[4096]{0:T(1024)S(1)} %bitcast.417), kind=kCustom, calls=%fused_computation.15 | custom fusion | flops 36864 | bytes 475136 | tf_op jit(solution)/shard_map/jvp()/scatter-add | solution.py:172
  240.2 10.7 %copy.115 = f32[3,2,128,128]{3,2,1,0:T(8,128)} copy(f32[3,2,128,128]{0,3,2,1:T(8,128)} %bitcast.410) | data formatting | bytes 786432
  250.8 2.5 fusion.31
  253.3 9.5 %copy.111 = f32[3,2,128,128]{0,3,2,1:T(8,128)} copy(f32[3,2,128,128]{3,2,1,0:T(8,128)} %fusion.31) | data formatting | bytes 786432 | tf_op jit(solution)/shard_map/jvp()/sub | solution.py:163
  262.9 8.6 %copy.112 = f32[3,2,128,128]{0,3,2,1:T(8,128)} copy(f32[3,2,128,128]{3,2,1,0:T(8,128)S(1)} %get-tuple-element.108) | data formatting | bytes 786432 | tf_op jit(solution)/shard_map/jvp()/slice | solution.py:133
  271.4 20.0 %gather_fusion.2 = f32[4096,3]{1,0:T(8,128)} fusion(f32[3,32768]{0,1:T(8,128)} %bitcast.415, s32[4096]{0:T(1024)S(1)} %get-tuple-element.72), kind=kCustom, calls=%fused_computation.2 | custom fusion | bytes 114688 | tf_op jit(solution)/shard_map/jvp()/gather | solution.py:168
  291.4 37.0 %scatter_custom_fusion.1 = f32[3,32768]{0,1:T(8,128)} fusion(f32[3,32768]{0,1:T(8,128)} %bitcast.411, s32[4096]{0:T(1024)} %bitcast.430, f32[4096,3]{1,0:T(8,128)} %gather_fusion.2, f32[4096,3]{1,0:T(8,128)S(1)} %gather_fusion, f32[4096]{0:T(1024)S(1)} %bitcast.425, f32[4096]{0:T(1024)S(1)} %bitcast.420, f32[4096]{0:T(1024)S(1)} %bitcast.418), kind=kCustom, calls=%fused_computation.13 | custom fusion | flops 73728 | bytes 2588672 | tf_op jit(solution)/shard_map/jvp()/scatter-add | solution.py:172
  328.4 10.6 %copy.116 = f32[3,2,128,128]{3,2,1,0:T(8,128)} copy(f32[3,2,128,128]{0,3,2,1:T(8,128)} %bitcast.412) | data formatting | bytes 786432
  339.0 4.6 %add_reduce_fusion = (f32[32,128]{1,0:T(8,128)S(1)}, f32[32,128]{1,0:T(8,128)S(1)}, f32[3,32]{0,1:T(8,128)S(1)}) fusion(f32[3,32,128]{0,2,1:T(8,128)} %bitcast.416, f32[3,32,128]{0,2,1:T(8,128)S(1)} %bitcast.413, f32[32,128]{1,0:T(8,128)S(1)} %get-tuple-element.116, f32[32,128]{1,0:T(8,128)S(1)} %get-tuple-element.117, f32[32,128]{1,0:T(8,128)S(1)} %and_select_fusion, ...), kind=kLoop, calls=%fused_computation.17 | loop fusion | flops 126880 | bytes 229760 | tf_op jit(solution)/shard_map/reduce_sum | solution.py:181
  343.7 0.2 fusion.157
  343.9 45.6 %all-reduce.4 = (f32[32,128]{1,0:T(8,128)S(1)}, f32[32,128]{1,0:T(8,128)S(1)}, f32[3,128]{1,0:T(4,128)S(1)}) all-reduce(f32[32,128]{1,0:T(8,128)S(1)} %get-tuple-element.55, f32[32,128]{1,0:T(8,128)S(1)} %get-tuple-element.54, f32[3,128]{1,0:T(4,128)S(1)} %fusion.157), channel_id=1, replica_groups=mesh['gx'=16,'gy'=16] {'gy'}, use_global_device_ids=true, to_apply=%region_3.4 | all-reduce | flops 8576 | bytes 68608 | tf_op jit(solution)/shard_map/psum | solution.py:203
  389.5 1.7 fusion.175
  391.4 1.7 fusion.174
  393.3 32.3 %all-reduce.5 = (f32[128]{0:T(128)S(1)}, f32[3,128]{1,0:T(4,128)}) all-reduce(f32[128]{0:T(128)S(1)} %copy-done.15, f32[3,128]{1,0:T(4,128)S(1)} %get-tuple-element.59), channel_id=1, replica_groups=mesh['gx'=16,'gy'=16] {'gx'}, use_global_device_ids=true, to_apply=%region_5.6 | all-reduce | flops 512 | bytes 4096 | tf_op jit(solution)/shard_map/psum | solution.py:187
  425.8 0.2 fusion.19
  426.2 0.6 slice_select_fusion.1
  427.0 0.6 slice_select_fusion
  427.8 0.6 constant_dynamic-slice_fusion.1
  428.3 0.6 constant_dynamic-slice_fusion
  (72 shorter events, 1.8 us)
Async XLA Ops:
  0.6 425.2 %copy-start = (f32[128]{0:T(128)S(1)}, f32[128]{0:T(128)}, u32[]{:S(2)}) copy-start(f32[128]{0:T(128)} %param.37) | copy-start | bytes 1540
  0.6 10.9 %copy-start.8 = (s32[32,128]{1,0:T(8,128)S(1)}, s32[32,128]{1,0:T(8,128)}, u32[]{:S(2)}) copy-start(s32[32,128]{1,0:T(8,128)} %param.29) | copy-start | bytes 49156
  0.7 11.5 %copy-start.12 = (f32[32,128]{1,0:T(8,128)S(1)}, f32[32,128]{1,0:T(8,128)}, u32[]{:S(2)}) copy-start(f32[32,128]{1,0:T(8,128)} %param.30) | copy-start | bytes 49156
  0.7 11.5 %copy-start.9 = (s32[32,128]{1,0:T(8,128)S(1)}, s32[32,128]{1,0:T(8,128)}, u32[]{:S(2)}) copy-start(s32[32,128]{1,0:T(8,128)} %param.31) | copy-start | bytes 49156
  5.6 12.7 %collective-permute-start.1 = (f32[8,2,1,128]{3,2,1,0:T(1,128)S(1)}, f32[8,2,1,128]{3,2,1,0:T(1,128)S(1)}, u32[]{:S(2)}, u32[]{:S(2)}) collective-permute-start(f32[8,2,1,128]{3,2,1,0:T(1,128)S(1)} %get-tuple-element.92), channel_id=1, source_target_pairs={{16,0},{32,16},{48,32},{64,48},{80,64},{96,80},{112,96},{128,112},... | collective-permute-start | bytes 24584 | tf_op jit(solution)/shard_map/ppermute | solution.py:24
  6.9 11.4 %collective-permute-start = (f32[8,2,1,128]{3,2,1,0:T(1,128)S(1)}, f32[8,2,1,128]{3,2,1,0:T(1,128)S(1)}, u32[]{:S(2)}, u32[]{:S(2)}) collective-permute-start(f32[8,2,1,128]{3,2,1,0:T(1,128)S(1)} %get-tuple-element.91), channel_id=1, source_target_pairs={{0,16},{16,32},{32,48},{48,64},{64,80},{80,96},{96,112},{112,128},... | collective-permute-start | bytes 24584 | tf_op jit(solution)/shard_map/ppermute | solution.py:23
  15.0 2.0 copy-start.17
  15.0 2.0 copy-start.19
  15.0 2.7 copy-start.2
  18.8 8.5 %copy-start.1 = (f32[32,128]{1,0:T(8,128)S(1)}, f32[32,128]{1,0:T(8,128)}, u32[]{:S(2)}) copy-start(f32[32,128]{1,0:T(8,128)} %param.28) | copy-start | bytes 49156
  19.4 77.5 %collective-permute-start.3 = (f32[8,2,130,1]{2,0,3,1:T(8,128)S(1)}, f32[8,2,130,1]{2,0,3,1:T(8,128)S(1)}, u32[]{:S(2)}, u32[]{:S(2)}) collective-permute-start(f32[8,2,130,1]{2,0,3,1:T(8,128)S(1)} %copy.106), channel_id=1, source_target_pairs={{1,0},{2,1},{3,2},{4,3},{5,4},{6,5},{7,6},{8,7},{9,8},{10,9},{11,1... | collective-permute-start | bytes 24968 | tf_op jit(solution)/shard_map/ppermute | solution.py:24
  25.1 72.2 %collective-permute-start.2 = (f32[8,2,130,1]{2,0,3,1:T(8,128)S(1)}, f32[8,2,130,1]{2,0,3,1:T(8,128)S(1)}, u32[]{:S(2)}, u32[]{:S(2)}) collective-permute-start(f32[8,2,130,1]{2,0,3,1:T(8,128)S(1)} %copy.105), channel_id=1, source_target_pairs={{0,1},{1,2},{2,3},{3,4},{4,5},{5,6},{6,7},{7,8},{8,9},{9,10},{10,1... | collective-permute-start | bytes 24968 | tf_op jit(solution)/shard_map/ppermute | solution.py:23
  101.9 1.2 copy-start.5
  104.2 1.8 copy-start.6
  104.2 1.8 copy-start.7
  180.6 23.0 %copy-start.11 = (f32[4096]{0:T(1024)S(1)}, f32[4096]{0:T(1024)}, u32[]{:S(2)}) copy-start(f32[4096]{0:T(1024)} %gather_fusion.3) | copy-start | bytes 49156
  240.2 10.7 %copy-start.4 = (f32[3,1,128,128]{3,2,1,0:T(8,128)S(1)}, f32[3,1,128,128]{3,2,1,0:T(8,128)}, u32[]{:S(2)}) copy-start(f32[3,1,128,128]{3,2,1,0:T(8,128)} %get-tuple-element.115) | copy-start | bytes 589828
  339.0 4.7 %copy-start.18 = (s32[32,1]{0,1:T(1,128)S(1)}, s32[32,1]{0,1:T(1,128)}, u32[]{:S(2)}) copy-start(s32[32,1]{0,1:T(1,128)} %param.36) | copy-start | bytes 388
  339.0 50.5 %copy-start.3 = (bf16[32,128,128]{2,1,0:T(8,128)(2,1)S(1)}, bf16[32,128,128]{2,1,0:T(8,128)(2,1)}, u32[]{:S(2)}) copy-start(bf16[32,128,128]{2,1,0:T(8,128)(2,1)} %minimum_convert_fusion) | copy-start | bytes 3145732
  339.0 52.4 %copy-start.10 = (f32[4096]{0:T(1024)S(1)}, f32[4096]{0:T(1024)}, u32[]{:S(2)}) copy-start(f32[4096]{0:T(1024)} %gather_fusion.5) | copy-start | bytes 49156
  343.6 49.6 %copy-start.15 = (f32[128]{0:T(128)S(1)}, f32[128]{0:T(128)}, u32[]{:S(2)}) copy-start(f32[128]{0:T(128)} %convolution_bitcast_fusion.1) | copy-start | bytes 1540
  343.6 82.2 %copy-start.14 = (f32[32]{0:T(128)S(1)}, f32[32]{0:T(128)}, u32[]{:S(2)}) copy-start(f32[32]{0:T(128)} %slice_reduce_fusion.2) | copy-start | bytes 388
  343.6 82.2 %copy-start.16 = (s32[32]{0:T(128)S(1)}, s32[32]{0:T(128)}, u32[]{:S(2)}) copy-start(s32[32]{0:T(128)} %param.33) | copy-start | bytes 388
  343.7 82.2 %copy-start.20 = (f32[32]{0:T(128)S(1)}, f32[32]{0:T(128)}, u32[]{:S(2)}) copy-start(f32[32]{0:T(128)} %param.35) | copy-start | bytes 388
  343.7 82.2 %copy-start.21 = (f32[32]{0:T(128)S(1)}, f32[32]{0:T(128)}, u32[]{:S(2)}) copy-start(f32[32]{0:T(128)} %param.34) | copy-start | bytes 388
  343.7 82.4 %copy-start.13 = (f32[32,128]{1,0:T(8,128)S(1)}, f32[32,128]{1,0:T(8,128)}, u32[]{:S(2)}) copy-start(f32[32,128]{1,0:T(8,128)} %param.32) | copy-start | bytes 49156
